TPU v7x, 512 devices: a whole 4x8x8 slice. The times are simulated.
512 devices in a mesh: row: 32 (over z, x), col: 16 (over y, core).
Axes of the slice: x: 4, y: 8, z: 8, core: 2. Of those that a mesh axis runs over, the one named last changes fastest.
Arguments:
- tokens: bfloat16 [4096, 6144], P('row', 'col'), may hold values from -6 to 6
- cotangent: bfloat16 [4096, 6144], P('row', 'col'), may hold values from -6 to 6
- w1_blocks: bfloat16 [32, 16, 2, 64, 64], P('row', 'col'), may hold values from -0.5 to 0.5
- w1_coords: int32 [32, 16, 2, 2], P('row', 'col'), may hold values from 0 to 23, as said below
- w1_count: int32 [32, 16], P('row', 'col'), may hold values from 1 to 2, as said below
- w2_blocks: bfloat16 [32, 16, 2, 64, 64], P('row', 'col'), may hold values from -0.5 to 0.5
- w2_coords: int32 [32, 16, 2, 2], P('row', 'col'), may hold values from 0 to 23, as said below
- w2_count: int32 [32, 16], P('row', 'col'), may hold values from 1 to 2, as said below
Outputs:
- input_grad: float32 [4096, 6144], P('row', 'col')
- w1_grad: float32 [32, 16, 2, 64, 64], P('row', 'col')
- w2_grad: float32 [32, 16, 2, 64, 64], P('row', 'col')
Inputs may be any that keep to these rules, and one draw needn't show every extreme that they name: `w1_coords`: the 2 coordinate pairs of a tile are distinct blocks inside that tile; only the first w1_count of them are live. `w1_count`: some tile has all 2 slots live in every draw. `w2_coords`: the 2 coordinate pairs of a tile are distinct blocks inside that tile; only the first w2_count of them are live. `w2_count`: some tile has all 2 slots live in every draw.
All inputs are finite; a program needn't handle non-finite values.
Results may differ from a plain program's by a relative error of at most 0.019.
Values may be sent and summed in bfloat16 or wider, within the bound.
A program may use at most 64 MiB of HBM per device.

v0:
```python
import math

import jax
import jax.numpy as jnp
from jax import lax
from jax.sharding import PartitionSpec as P

FF = 24576


def gelu_pair(hidden):
    inner = 0.7978845608028654 * (hidden + 0.044715 * hidden * hidden * hidden)
    tanh_term = jnp.tanh(inner)
    gelu_out = 0.5 * hidden * (1.0 + tanh_term)
    gelu_slope = 0.5 * (1.0 + tanh_term) + 0.5 * hidden * (
        1.0 - tanh_term * tanh_term
    ) * 0.7978845608028654 * (1.0 + 3.0 * 0.044715 * hidden * hidden)
    return (gelu_out, gelu_slope)


def pick_blocks(operand, block_index, block_size):
    return jnp.take(operand.reshape(operand.shape[0], -1, block_size), block_index, axis=1)


def place_blocks(products, block_index, out_blocks):
    tok_count = products.shape[1]
    block_size = products.shape[2]
    empty = jnp.zeros((tok_count, out_blocks, block_size), jnp.float32)
    placed = empty.at[:, block_index, :].add(jnp.transpose(products, (1, 0, 2)))
    return placed.reshape(tok_count, out_blocks * block_size)


def strip_layout(strip_blocks, strip_coords, strip_count, row_band):
    group_count = strip_blocks.shape[0]
    num_slots = strip_blocks.shape[2]
    block_size = strip_blocks.shape[-1]
    flat_blocks = strip_blocks.reshape(-1, block_size, block_size)
    coord_pairs = strip_coords.reshape(-1, 2)
    tile_index = jnp.repeat(jnp.arange(group_count, dtype=jnp.int32), num_slots)
    slot_index = jnp.tile(jnp.arange(num_slots, dtype=jnp.int32), group_count)
    is_live = (slot_index < jnp.repeat(strip_count.reshape(-1), num_slots)).astype(jnp.float32)
    return (flat_blocks, coord_pairs[:, 0], coord_pairs[:, 1], tile_index * row_band, is_live)


def shards(tokens, cotangent, w1_blocks, w1_coords, w1_count, w2_blocks, w2_coords, w2_count):
    block_size = w1_blocks.shape[-1]
    num_slots = w1_blocks.shape[2]
    tok_rows = tokens.shape[0]
    row_count = lax.axis_size("row")
    col_count = lax.axis_size("col")
    model_width = tokens.shape[1] * col_count
    row_band = model_width // row_count // block_size
    hidden_band = FF // col_count // block_size
    first_blocks, first_coords, first_count = (
        lax.all_gather(w1_blocks, "row", axis=0, tiled=True),
        lax.all_gather(w1_coords, "row", axis=0, tiled=True),
        lax.all_gather(w1_count, "row", axis=0, tiled=True),
    )
    second_blocks, second_coords, second_count = (
        lax.all_gather(w2_blocks, "row", axis=0, tiled=True),
        lax.all_gather(w2_coords, "row", axis=0, tiled=True),
        lax.all_gather(w2_count, "row", axis=0, tiled=True),
    )
    blocks_one, row_one, col_one, base_one, live_one = strip_layout(
        first_blocks, first_coords, first_count, row_band
    )
    blocks_two, row_two, col_two, base_two, live_two = strip_layout(
        second_blocks, second_coords, second_count, row_band
    )
    model_one = base_one + row_one
    model_two = base_two + col_two
    features, upstream_full = (
        lax.all_gather(tokens, "col", axis=1, tiled=True),
        lax.all_gather(cotangent, "col", axis=1, tiled=True),
    )
    feat_blocks = pick_blocks(features, model_one, block_size)
    pre_blocks = (
        jnp.einsum("tnb,nbc->ntc", feat_blocks, blocks_one, preferred_element_type=jnp.float32)
        * live_one[:, None, None]
    )
    hidden = place_blocks(pre_blocks, col_one, hidden_band)
    gelu_out, gelu_slope = gelu_pair(hidden)
    active = gelu_out.astype(jnp.bfloat16)
    act_blocks = pick_blocks(active, row_two, block_size)
    up_blocks = pick_blocks(upstream_full, model_two, block_size)
    back_blocks = (
        jnp.einsum("tnc,nbc->ntb", up_blocks, blocks_two, preferred_element_type=jnp.float32)
        * live_two[:, None, None]
    )
    grad_two = (
        jnp.einsum("tnb,tnc->nbc", act_blocks, up_blocks, preferred_element_type=jnp.float32)
        * live_two[:, None, None]
    )
    upstream = place_blocks(back_blocks, row_two, hidden_band)
    hidden_grad = (upstream * gelu_slope).astype(jnp.bfloat16)
    grad_blocks = pick_blocks(hidden_grad, col_one, block_size)
    back_one = (
        jnp.einsum("tnc,nbc->ntb", grad_blocks, blocks_one, preferred_element_type=jnp.float32)
        * live_one[:, None, None]
    )
    partial_input = place_blocks(back_one, model_one, model_width // block_size)
    input_grad = lax.psum_scatter(
        partial_input.astype(jnp.bfloat16), "col", scatter_dimension=1, tiled=True
    ).astype(jnp.float32)
    grad_one = (
        jnp.einsum("tnb,tnc->nbc", feat_blocks, grad_blocks, preferred_element_type=jnp.float32)
        * live_one[:, None, None]
    )
    strip_shape = (row_count, 1, num_slots, block_size, block_size)
    total_one, total_two = (
        lax.psum_scatter(
            grad_one.reshape(strip_shape).astype(jnp.bfloat16),
            "row",
            scatter_dimension=0,
            tiled=True,
        ).astype(jnp.float32),
        lax.psum_scatter(
            grad_two.reshape(strip_shape).astype(jnp.bfloat16),
            "row",
            scatter_dimension=0,
            tiled=True,
        ).astype(jnp.float32),
    )
    grad_scale = 1.0 / math.sqrt(tok_rows * row_count)
    return (input_grad, total_one * grad_scale, total_two * grad_scale)


def solution(mesh):
    return jax.shard_map(
        shards,
        mesh=mesh,
        in_specs=(
            P("row", "col"),
            P("row", "col"),
            P("row", "col", None, None, None),
            P("row", "col", None, None),
            P("row", "col"),
            P("row", "col", None, None, None),
            P("row", "col", None, None),
            P("row", "col"),
        ),
        out_specs=(
            P("row", "col"),
            P("row", "col", None, None, None),
            P("row", "col", None, None, None),
        ),
        check_vma=False,
    )
```

profile of v0, /device:TPU:29, one launch (start us, length us, event | category | flops | bytes accessed | tf_op | source)
XLA Modules:
  0.0 764.5 jit_solution(7136176293204711522)
XLA Ops:
  7.2 1.6 copy.30
  8.9 1.6 copy.29
  12.0 1.3 dynamic-slice
  13.2 0.7 bitcast_dynamic-update-slice_fusion
  13.9 0.7 bitcast_dynamic-update-slice_fusion.1
  14.6 19.7 %all-reduce.2 = (s32[32]{0:T(128)S(1)}, s32[32]{0:T(128)S(1)}) all-reduce(s32[32]{0:T(128)S(1)} %bitcast_dynamic-update-slice_fusion, s32[32]{0:T(128)S(1)} %bitcast_dynamic-update-slice_fusion.1), channel_id=1, replica_groups=mesh['row'=32,'col'=16] {'row'}, use_global_device_ids=true, to_apply=%add.1 | all-reduce | flops 64 | bytes 512
  34.8 33.8 %all_gather.25 = s32[32,1,2,2]{3,2,1,0:T(2,128)S(1)} all-gather(s32[1,1,2,2]{3,2,1,0:T(2,128)} %param.18), channel_id=1, replica_groups=mesh['row'=32,'col'=16] {'row'}, dimensions={0}, use_global_device_ids=true | all-gather | bytes 528 | tf_op jit(solution)/shard_map/all_gather | solution.py:61
  68.8 32.8 %all_gather.24 = s32[32,1,2,2]{3,2,1,0:T(2,128)S(1)} all-gather(s32[1,1,2,2]{3,2,1,0:T(2,128)} %param.15), channel_id=1, replica_groups=mesh['row'=32,'col'=16] {'row'}, dimensions={0}, use_global_device_ids=true | all-gather | bytes 528 | tf_op jit(solution)/shard_map/all_gather | solution.py:56
  101.9 41.4 %all_gather.30 = bf16[32,1,2,64,64]{4,3,2,1,0:T(8,128)(2,1)} all-gather(bf16[1,1,2,64,64]{4,3,2,1,0:T(8,128)(2,1)} %param.14), channel_id=1, replica_groups=mesh['row'=32,'col'=16] {'row'}, dimensions={0}, use_global_device_ids=true | all-gather | bytes 540672 | tf_op jit(solution)/shard_map/all_gather | solution.py:55
  143.3 41.3 %all_gather.27 = bf16[32,1,2,64,64]{4,3,2,1,0:T(8,128)(2,1)} all-gather(bf16[1,1,2,64,64]{4,3,2,1,0:T(8,128)(2,1)S(1)} %copy-done.4), channel_id=1, replica_groups=mesh['row'=32,'col'=16] {'row'}, dimensions={0}, use_global_device_ids=true | all-gather | bytes 540672 | tf_op jit(solution)/shard_map/all_gather | solution.py:60
  184.7 3.1 gather_fusion.1
  187.8 2.2 gather_fusion
  189.9 1.0 copy-done.2
  190.9 1.7 convolution_multiply_fusion.2
  192.7 3.7 scatter_fusion
  196.5 3.6 convolution_multiply_fusion.1
  200.1 7.0 scatter_fusion.1
  207.1 0.6 multiply_convert_fusion.2
  207.7 0.7 gather_fusion.3
  208.9 1.7 multiply_convert_fusion
  210.8 0.7 gather_fusion.2
  212.0 1.7 multiply_convert_fusion.1
  213.9 1.8 convolution_multiply_fusion
  216.2 7.0 scatter_fusion.2
  223.2 1.5 convert_element_type.76
  224.7 241.4 %reduce-scatter.8.cloned.1.call-done = bf16[1,1,2,64,64]{4,3,2,1,0:T(8,128)(2,1)} async-done(((bf16[32,1,2,64,64]{4,3,2,1,0:T(8,128)(2,1)}), bf16[1,1,2,64,64]{4,3,2,1,0:T(8,128)(2,1)}) %reduce-scatter.8.cloned.1.call-update) | async-done | bytes 16400 | tf_op jit(solution)/shard_map/reduce_scatter | solution.py:117
  466.1 1.4 convert_multiply_fusion
  467.5 221.1 %reduce-scatter.6.cloned.1.call-done = bf16[1,1,2,64,64]{4,3,2,1,0:T(8,128)(2,1)} async-done(((bf16[32,1,2,64,64]{4,3,2,1,0:T(8,128)(2,1)}), bf16[1,1,2,64,64]{4,3,2,1,0:T(8,128)(2,1)}) %reduce-scatter.6.cloned.1.call-update) | async-done | bytes 16400 | tf_op jit(solution)/shard_map/reduce_scatter | solution.py:111
  688.6 1.4 convert_multiply_fusion.1
  690.0 66.3 %reduce-scatter.10.cloned.1.call-done = bf16[384,128]{1,0:T(8,128)(2,1)} async-done(((bf16[6144,128]{1,0:T(8,128)(2,1)}), bf16[384,128]{1,0:T(8,128)(2,1)}) %reduce-scatter.10.cloned.1.call-update) | async-done | bytes 98320
  756.2 1.0 copy.40
  757.3 0.7 convert_element_type.78
  (51 shorter events, 2.9 us)
Async XLA Ops:
  7.2 136.1 %copy-start.4 = (bf16[1,1,2,64,64]{4,3,2,1,0:T(8,128)(2,1)S(1)}, bf16[1,1,2,64,64]{4,3,2,1,0:T(8,128)(2,1)}, u32[]{:S(2)}) copy-start(bf16[1,1,2,64,64]{4,3,2,1,0:T(8,128)(2,1)} %param.17) | copy-start | bytes 49156
  7.2 177.5 %all-gather.5.cloned.1.call-start = ((), (), s32[]{:S(2)}) async-start(), calls=%async_computation.4 | async-start | bytes 1671168 | tf_op jit(solution)/shard_map/all_gather | solution.py:73
  8.9 178.9 %all-gather.3.cloned.1.call-start = ((), (), s32[]{:S(2)}) async-start(), calls=%async_computation.3 | async-start | bytes 1671168 | tf_op jit(solution)/shard_map/all_gather | solution.py:74
  10.6 455.5 %reduce-scatter.8.cloned.1.call-start = ((), (), s32[]{:S(2)}) async-start(), calls=%async_computation.6 | async-start | bytes 1081344 | tf_op jit(solution)/shard_map/reduce_scatter | solution.py:117
  189.9 1.0 copy-start.2
  207.7 1.2 copy-start.3
  210.7 477.9 %reduce-scatter.6.cloned.1.call-start = ((), (), s32[]{:S(2)}) async-start(), calls=%async_computation.5 | async-start | bytes 1081344 | tf_op jit(solution)/shard_map/reduce_scatter | solution.py:111
  210.8 1.2 copy-start.1
  212.0 1.9 copy-start
  213.8 542.5 %reduce-scatter.10.cloned.1.call-start = ((), (), s32[]{:S(2)}) async-start(), calls=%async_computation.7 | async-start | bytes 1671168
Sparse Core Ops, SparseCore 0:
  10.7 46.0 all-gather.4
  58.9 40.4 all-gather.2
  210.8 255.2 reduce-scatter.7
  470.4 218.1 reduce-scatter.5
  691.3 64.9 reduce-scatter.9
where the time goes:
time: 766 us; the launch traced here: 764 us
  waiting for transfers between devices  529 us (69%)
  blocking collectives  169 us (22%)
  other arithmetic  23.6 us (3%)
  local copies, waits for them, and re-layouts  16.9 us (2%)
  between operations  15.3 us (2%)
  matrix products  10.6 us (1%)
    reduce_scatter x1, waiting for transfers between devices, shards(): lax.psum_scatter(grad_two.reshape(strip_shape).astype(jnp.bfloat16), 'row...  241 us
    reduce_scatter x1, waiting for transfers between devices, shards(): lax.psum_scatter(grad_one.reshape(strip_shape).astype(jnp.bfloat16), 'row...  221 us
    unnamed x6, waiting for transfers between devices  66.3 us
    all_gather x1, blocking collectives, shards(): lax.all_gather(w1_blocks, 'row', axis=0, tiled=True)  41.4 us
    all_gather x1, blocking collectives, shards(): lax.all_gather(w2_blocks, 'row', axis=0, tiled=True)  41.3 us
    all_gather x1, blocking collectives, shards(): lax.all_gather(w2_coords, 'row', axis=0, tiled=True)  33.8 us
    all_gather x1, blocking collectives, shards(): lax.all_gather(w1_coords, 'row', axis=0, tiled=True)  32.8 us
    unnamed x1, blocking collectives  19.7 us
  transfers between devices with their start and end apart: 5, of which 3 were waited for; matrix products, arithmetic and copies ran while one was open for 3% of the time, Pallas kernels for 0%

commit v1 on v0

v1 whole, which is shorter than its diff:
```python
import functools
import math

import jax
import jax.numpy as jnp
from jax import lax
from jax.experimental import pallas as pl
from jax.experimental.pallas import tpu as pltpu
from jax.sharding import PartitionSpec as P

MESH = pl.DeviceIdType.MESH
F32 = jnp.float32
BF16 = jnp.bfloat16
NT = (((1,), (1,)), ((), ()))
NN = (((1,), (0,)), ((), ()))
TN = (((0,), (0,)), ((), ()))
NZ, NX, NY = 8, 4, 8
BLK = 64
DEAD = -64

FAMILIES = (
    ("right", 8), ("left", 8), ("pair", 16), ("wx", 3), ("mx", 3), ("wzr", 4), ("wzl", 4),
    ("mzr", 4), ("mzl", 3), ("part", 8), ("cr", 4), ("cl", 4), ("gx", 24), ("gz", 7),
)
BASE = {}
TOTAL = 0
for family, amount in FAMILIES:
    BASE[family] = TOTAL
    TOTAL += amount


def gelu_pair(hidden):
    inner = 0.7978845608028654 * (hidden + 0.044715 * hidden * hidden * hidden)
    tanh_term = jnp.tanh(inner)
    gelu_out = 0.5 * hidden * (1.0 + tanh_term)
    gelu_slope = 0.5 * (1.0 + tanh_term) + 0.5 * hidden * (
        1.0 - tanh_term * tanh_term
    ) * 0.7978845608028654 * (1.0 + 3.0 * 0.044715 * hidden * hidden)
    return (gelu_out, gelu_slope)


def kernel(
    scale, tok, cot, wpk, meta, ig, wg,
    xc, wall, mall, a1, a2, hid, ups, act, grd, part, psib, ssum, rbr, rbl,
    gr, xr, zs, zr, mv, dv, ms, md, send_sems, recv_sems, local_sems,
):
    row, col = lax.axis_index("row"), lax.axis_index("col")
    z, x, y, core = row // NX, row % NX, col // 2, col % 2

    def dev(dz=0, dx=0, dy=0, other=False):
        there = (1 - core) if other else core
        return ((z + dz) % NZ * NX + (x + dx) % NX, (y + dy) % NY * 2 + there)

    sibling = dev(other=True)
    right, left = dev(dy=1), dev(dy=NY - 1)
    z_right, z_left = dev(dz=1), dev(dz=NZ - 1)

    barrier = pltpu.get_barrier_semaphore()
    partners = [sibling, right, left]
    partners += [dev(dx=e) for e in range(1, NX)]
    partners += [dev(dz=e) for e in range(1, NZ)]
    for partner in partners:
        pl.semaphore_signal(barrier, inc=1, device_id=partner, device_id_type=MESH)

    pending = []

    def describe(family, n, src, dst, target):
        slot = BASE[family] + n
        return pltpu.make_async_remote_copy(
            src_ref=src, dst_ref=dst, send_sem=send_sems.at[slot], recv_sem=recv_sems.at[slot],
            device_id=target, device_id_type=MESH,
        )

    def send(family, n, src, dst, target):
        copy = describe(family, n, src, dst, target)
        copy.start()
        pending.append(copy)

    def arrived(family, n, dst):
        describe(family, n, dst, dst, sibling).wait_recv()

    def shard(dy, other=False):
        return (y + dy) % NY * 2 + ((1 - core) if other else core)

    own = (tok, cot)
    xc[col, 0] = tok[...]
    xc[col, 1] = cot[...]
    wall[z, x] = wpk[...]
    mall[row] = meta[...]
    hid[0] = jnp.zeros((BLK, 128), F32)
    ups[0] = jnp.zeros((BLK, 128), F32)
    pl.semaphore_wait(barrier, len(partners))

    for e in range(1, NX):
        send("mx", e - 1, meta, mall.at[row], dev(dx=e))
        send("wx", e - 1, wpk, wall.at[z, x], dev(dx=e))
    for j in range(2):
        send("right", j, own[j], xc.at[col, j], right)
        send("left", j, own[j], xc.at[col, j], left)
    for j in range(2):
        send("pair", j, own[j], xc.at[col, j], sibling)
    for e in range(1, NX):
        there = (x + NX - e) % NX
        arrived("mx", e - 1, mall.at[z * NX + there])
        arrived("wx", e - 1, wall.at[z, there])

    def plane(dz):
        return (z + dz) % NZ

    def tiles_on(d):
        back, ahead = plane(NZ - d + 1), plane(d - 1)
        if d <= 3:
            send("mzr", d - 1, mall.at[pl.ds(back * NX, NX)], mall.at[pl.ds(back * NX, NX)], z_right)
            send("mzl", d - 1, mall.at[pl.ds(ahead * NX, NX)], mall.at[pl.ds(ahead * NX, NX)], z_left)
            send("wzr", d - 1, wall.at[back], wall.at[back], z_right)
            send("wzl", d - 1, wall.at[ahead], wall.at[ahead], z_left)
        else:
            send("mzr", d - 1, mall.at[pl.ds(back * NX, NX)], mall.at[pl.ds(back * NX, NX)], z_right)
            send("wzr", d - 1, wall.at[back, pl.ds(0, 2)], wall.at[back, pl.ds(0, 2)], z_right)
            send("wzl", d - 1, wall.at[ahead, pl.ds(2, 2)], wall.at[ahead, pl.ds(2, 2)], z_left)

    def tiles_in(d):
        back, ahead = plane(NZ - d), plane(d)
        arrived("mzr", d - 1, mall.at[pl.ds(back * NX, NX)])
        if d <= 3:
            arrived("mzl", d - 1, mall.at[pl.ds(ahead * NX, NX)])
            arrived("wzr", d - 1, wall.at[back])
            arrived("wzl", d - 1, wall.at[ahead])
            tiles_on(d + 1)
        else:
            arrived("wzr", d - 1, wall.at[back, pl.ds(0, 2)])
            arrived("wzl", d - 1, wall.at[ahead, pl.ds(2, 2)])

    def acts_in(d, j):
        if d <= 3 or j == 0:
            here = xc.at[shard(NY - d), j]
            arrived("right", 2 * (d - 1) + j, here)
            if d < 3 or (d == 3 and j == 0):
                send("right", 2 * d + j, here, here, right)
            send("pair", 2 * (NY - d) + j, here, here, sibling)
        if d <= 3 or j == 1:
            here = xc.at[shard(d), j]
            arrived("left", 2 * (d - 1) + j, here)
            if d < 3 or (d == 3 and j == 1):
                send("left", 2 * d + j, here, here, left)
            send("pair", 2 * d + j, here, here, sibling)

    tiles_on(1)
    for d in range(1, 4):
        acts_in(d, 0)
        acts_in(d, 1)
        tiles_in(d)
    tiles_in(4)
    acts_in(4, 0)
    acts_in(4, 1)
    for dy in range(NY):
        for j in range(2):
            arrived("pair", 2 * dy + j, xc.at[shard(dy, True), j])

    table = mall[:, 0, :]
    mv[...] = table
    rows = lax.broadcasted_iota(jnp.int32, (32, 128), 0)
    lanes = lax.broadcasted_iota(jnp.int32, (32, 128), 1)
    derived = jnp.zeros((32, 128), jnp.int32)
    for matrix, first in ((0, 2), (1, 6)):
        cols = [
            jnp.sum(jnp.where(lanes == first + k, table, 0), axis=1, keepdims=True) for k in range(2)
        ]
        flat = jnp.sum(
            jnp.where(rows == lanes // 2, jnp.where(lanes % 2 == 0, cols[0], cols[1]), 0),
            axis=0, keepdims=True,
        )
        for k in range(2):
            same = (flat == cols[k]) & (lanes < 2 * rows + k)
            before = jnp.max(jnp.where(same, lanes + 1, 0), axis=1, keepdims=True)
            derived = jnp.where(lanes == 2 * matrix + k, before, derived)
        ends = jnp.max(jnp.where((flat == rows) & (lanes < 64), lanes + 1, 0), axis=1, keepdims=True)
        derived = jnp.where(lanes == 4 + matrix, ends, derived)
    dv[...] = derived
    copies = [
        pltpu.make_async_copy(mv, ms, local_sems.at[0]),
        pltpu.make_async_copy(dv, md, local_sems.at[1]),
    ]
    for copy in copies:
        copy.start()
    for copy in copies:
        copy.wait()

    lane = lax.broadcasted_iota(jnp.int32, (1, 128), 1)
    low = lane < BLK
    high = jnp.where(low, 0, 1)

    def places(c, first):
        found = []
        for i in range(2):
            for k in range(2):
                place = ms[2 * c + i, first + k] + 3 * i
                found.append([(high + 2 * t) == place for t in range(3)])
        return found

    def forward(c, carry):
        ones, twos = places(c, 0), places(c, 4)
        for i in range(2):
            pack = wall[c // 2, (c % 2) * 2 + i].astype(F32)
            turned = pltpu.roll(pack, BLK, 1)
            first = jnp.where(low, pack, turned)
            second = jnp.where(low, turned, pack)
            for k in range(2):
                n = 2 * i + k
                for t in range(3):
                    span = pl.ds(128 * t, 128)
                    a1[c, pl.ds(BLK * n, BLK), span] = jnp.where(
                        ones[n][t], first[BLK * k : BLK * (k + 1)], 0.0
                    ).astype(BF16)
                    a2[pl.ds(BLK * n, BLK), span] = jnp.where(
                        twos[n][t], second[BLK * k : BLK * (k + 1)], 0.0
                    ).astype(BF16)
        pre = lax.dot_general(a1[c], xc[c, 0], NT, preferred_element_type=F32)
        back = lax.dot_general(a2[...], xc[c, 1], NT, preferred_element_type=F32)
        for n in range(4):
            k = n % 2
            r = 2 * c + n // 2
            hid[1 + 4 * c + n] = pre[BLK * n : BLK * (n + 1)] + hid[md[r, k]]
            ups[1 + 4 * c + n] = back[BLK * n : BLK * (n + 1)] + ups[md[r, 2 + k]]
        return carry

    lax.fori_loop(0, 16, forward, 0)

    def middle(q, carry):
        gelu_out, gelu_slope = gelu_pair(hid[md[q, 4]])
        act[q] = gelu_out.astype(BF16)
        grd[q] = (ups[md[q, 5]] * gelu_slope).astype(BF16)
        return carry

    lax.fori_loop(0, 24, middle, 0)

    def pick(product, found):
        total = jnp.where(found[0], product[:, 0:128], 0.0)
        for t in range(1, 3):
            total = total + jnp.where(found[t], product[:, 128 * t : 128 * (t + 1)], 0.0)
        return total + pltpu.roll(total, BLK, 1)

    def backward(c):
        ones, twos = places(c, 0), places(c, 4)
        slots = [(2 * c + n // 2, n % 2) for n in range(4)]
        grads = jnp.concatenate([grd[ms[r, 2 + k]] for r, k in slots], axis=0)
        acts = jnp.concatenate([act[ms[r, 6 + k]] for r, k in slots], axis=0)
        part[c] = lax.dot_general(grads, a1[c], TN, preferred_element_type=F32).astype(BF16)
        one = lax.dot_general(grads, xc[c, 0], NN, preferred_element_type=F32)
        two = lax.dot_general(acts, xc[c, 1], NN, preferred_element_type=F32)
        for n in range(4):
            span = slice(BLK * n, BLK * (n + 1))
            both = jnp.where(low, pick(one[span], ones[n]), pick(two[span], twos[n]))
            gr[c // 2, (c % 2) * 2 + n // 2, pl.ds(BLK * (n % 2), BLK), :] = both.astype(BF16)

    def settle(dy):
        there = (y + dy) % NY
        arrived("part", dy, psib.at[there])
        total = part[shard(dy)].astype(F32) + psib[there].astype(F32)
        if dy == 4:
            ssum[there] = total.astype(BF16)
            send("cr", 0, ssum.at[there, pl.ds(0, 64)], rbr.at[0, pl.ds(0, 64)], right)
            send("cl", 0, ssum.at[there, pl.ds(64, 64)], rbl.at[0, pl.ds(64, 64)], left)
        elif dy == 3:
            arrived("cr", 0, rbr.at[0, pl.ds(0, 64)])
            ssum[there, pl.ds(0, 64)] = (total[:64] + rbr[0, pl.ds(0, 64)].astype(F32)).astype(BF16)
            ssum[there, pl.ds(64, 64)] = total[64:].astype(BF16)
            send("cr", 1, ssum.at[there], rbr.at[1], right)
        elif dy == 5:
            arrived("cl", 0, rbl.at[0, pl.ds(64, 64)])
            ssum[there, pl.ds(0, 64)] = total[:64].astype(BF16)
            ssum[there, pl.ds(64, 64)] = (total[64:] + rbl[0, pl.ds(64, 64)].astype(F32)).astype(BF16)
            send("cl", 1, ssum.at[there], rbl.at[1], left)
        elif dy in (1, 2):
            arrived("cr", 3 - dy, rbr.at[3 - dy])
            ssum[there] = (total + rbr[3 - dy].astype(F32)).astype(BF16)
            send("cr", 4 - dy, ssum.at[there], rbr.at[4 - dy], right)
        elif dy in (6, 7):
            arrived("cl", dy - 5, rbl.at[dy - 5])
            ssum[there] = (total + rbl[dy - 5].astype(F32)).astype(BF16)
            send("cl", dy - 4, ssum.at[there], rbl.at[dy - 4], left)
        else:
            arrived("cr", 3, rbr.at[3])
            arrived("cl", 3, rbl.at[3])
            ig[...] = total + rbr[3].astype(F32) + rbl[3].astype(F32)

    before = None
    for dy in (4, 3, 5, 2, 6, 1, 7, 0):
        there = (y + dy) % NY

        def both_cores(cc, carry, there=there):
            backward(there * 2 + cc)
            return carry

        lax.fori_loop(0, 2, both_cores, 0)
        send("part", dy, part.at[shard(dy, True)], psib.at[there], sibling)
        for e in range(1, NX):
            send("gx", there * 3 + e - 1, gr.at[there, (x + e) % NX], xr.at[there, e - 1], dev(dx=e))
        if before is not None:
            settle(before)
        before = dy

    def plane_sum(there):
        total = gr[there, x].astype(F32)
        for e in range(1, NX):
            arrived("gx", there * 3 + e - 1, xr.at[there, e - 1])
            total = total + xr[there, e - 1].astype(F32)
        return total

    for e in range(1, NZ):
        there = plane(e)
        zs[there] = plane_sum(there).astype(BF16)
        send("gz", e - 1, zs.at[there], zr.at[e - 1], dev(dz=e))
    settle(before)
    total = plane_sum(z)
    for e in range(1, NZ):
        arrived("gz", e - 1, zr.at[e - 1])
        total = total + zr[e - 1].astype(F32)
    wg[...] = total * scale

    for copy in pending:
        copy.wait_send()


def shards(tokens, cotangent, w1_blocks, w1_coords, w1_count, w2_blocks, w2_coords, w2_count):
    one = w1_blocks.reshape(2, BLK, BLK)
    two = w2_blocks.reshape(2, BLK, BLK)
    pack = jnp.concatenate(
        [jnp.swapaxes(one, 1, 2).reshape(2 * BLK, BLK), two.reshape(2 * BLK, BLK)], axis=1
    )
    slot = jnp.arange(2, dtype=jnp.int32)
    c1, c2 = w1_coords.reshape(2, 2), w2_coords.reshape(2, 2)
    facts = jnp.concatenate([
        jnp.where(slot < w1_count.reshape(1), c1[:, 0], DEAD), c1[:, 1],
        jnp.where(slot < w2_count.reshape(1), c2[:, 1], DEAD), c2[:, 0],
    ])
    meta = jnp.broadcast_to(jnp.pad(facts, (0, 120))[None, :], (8, 128))
    scale = 1.0 / math.sqrt(4096)
    shard = (128, 384)
    vmem = pl.BlockSpec(memory_space=pltpu.VMEM)
    input_grad, grads = pl.pallas_call(
        functools.partial(kernel, scale),
        out_shape=(
            jax.ShapeDtypeStruct(shard, F32),
            jax.ShapeDtypeStruct((128, 128), F32),
        ),
        in_specs=[vmem] * 4,
        out_specs=(vmem, vmem),
        scratch_shapes=[
            pltpu.VMEM((16, 2) + shard, BF16),
            pltpu.VMEM((NZ, NX, 128, 128), BF16),
            pltpu.VMEM((32, 8, 128), jnp.int32),
            pltpu.VMEM((16, 256, 384), BF16),
            pltpu.VMEM((256, 384), BF16),
            pltpu.VMEM((65, BLK, 128), F32),
            pltpu.VMEM((65, BLK, 128), F32),
            pltpu.VMEM((24, BLK, 128), BF16),
            pltpu.VMEM((24, BLK, 128), BF16),
            pltpu.VMEM((16,) + shard, BF16),
            pltpu.VMEM((8,) + shard, BF16),
            pltpu.VMEM((8,) + shard, BF16),
            pltpu.VMEM((4,) + shard, BF16),
            pltpu.VMEM((4,) + shard, BF16),
            pltpu.VMEM((NZ, NX, 128, 128), BF16),
            pltpu.VMEM((NZ, 3, 128, 128), BF16),
            pltpu.VMEM((NZ, 128, 128), BF16),
            pltpu.VMEM((7, 128, 128), BF16),
            pltpu.VMEM((32, 128), jnp.int32),
            pltpu.VMEM((32, 128), jnp.int32),
            pltpu.SMEM((32, 128), jnp.int32),
            pltpu.SMEM((32, 128), jnp.int32),
            pltpu.SemaphoreType.DMA((TOTAL,)),
            pltpu.SemaphoreType.DMA((TOTAL,)),
            pltpu.SemaphoreType.DMA((2,)),
        ],
        compiler_params=pltpu.CompilerParams(
            collective_id=0, has_side_effects=True, vmem_limit_bytes=40 * 1024 * 1024
        ),
        cost_estimate=pl.CostEstimate(
            flops=16 * 5 * 2 * 256 * 384 * 128, bytes_accessed=1 << 20, transcendentals=24 * 64 * 128
        ),
    )(tokens, cotangent, pack, meta)
    grad_one = jnp.swapaxes(grads[:, :BLK].reshape(2, BLK, BLK), 1, 2).reshape(w1_blocks.shape)
    grad_two = grads[:, BLK:].reshape(w2_blocks.shape)
    return (input_grad, grad_one, grad_two)


def solution(mesh):
    wide = P("row", "col", None, None, None)
    return jax.shard_map(
        shards,
        mesh=mesh,
        in_specs=(
            P("row", "col"), P("row", "col"),
            wide, P("row", "col", None, None), P("row", "col"),
            wide, P("row", "col", None, None), P("row", "col"),
        ),
        out_specs=(P("row", "col"), wide, wide),
        check_vma=False,
    )
```

time: 766 us -> 78.1 us (0.10)
  the two profiles are of different devices: /device:TPU:29 before, /device:TPU:4 now
where the time goes in v1:
time: 78.1 us; the launch traced here: 77.9 us
  Pallas kernels  70.9 us (91%)
  local copies, waits for them, and re-layouts  3.99 us (5%)
  between operations  2 us (3%)
  other arithmetic  0.93 us (1%)
    pallas_call x1, Pallas kernels, shards(): pl.pallas_call(functools.partial(kernel, scale), out_shape=(jax.ShapeDtyp...  70.9 us

profile of v1, /device:TPU:4, one launch (start us, length us, event | category | flops | bytes accessed | tf_op | source)
XLA Modules:
  0.0 77.9 jit_solution(9386674465974852840)
XLA Ops:
  1.9 0.0 copy-start.2
  1.9 0.0 copy-start.3
  1.9 0.0 copy-start.1
  2.0 0.7 copy-done.2
  2.6 0.0 copy-start
  2.6 0.2 slice_reduce_fusion.3
  2.8 0.0 copy-done.3
  2.8 0.2 slice_reduce_fusion.1
  3.0 0.1 pad_add_fusion
  3.1 0.9 %copy.13 = bf16[2,64,64]{2,1,0:T(8,128)(2,1)S(1)} copy(bf16[2,64,64]{1,2,0:T(8,128)(2,1)} %bitcast.21) | data formatting | bytes 32768 | tf_op jit(solution)/shard_map/transpose | solution.py:329
  3.9 0.8 %pad_maximum_fusion.wpk = bf16[128,128]{1,0:T(8,128)(2,1)S(1)} fusion(bf16[128,64]{1,0:T(8,128)(2,1)} %bitcast.20, bf16[128,64]{1,0:T(8,128)(2,1)S(1)} %bitcast.17), kind=kLoop, calls=%fused_computation | loop fusion | flops 65536 | bytes 65536 | tf_op jit(solution)/shard_map/concatenate | solution.py:328
  4.8 0.0 copy-done.1
  4.8 0.0 copy-done
  4.8 70.9 %shard_map.103 = (f32[128,384]{1,0:T(8,128)S(1)}, f32[128,128]{1,0:T(8,128)S(1)}) custom-call(bf16[128,384]{1,0:T(8,128)(2,1)S(1)} %copy-done, bf16[128,384]{1,0:T(8,128)(2,1)S(1)} %copy-done.1, bf16[128,128]{1,0:T(8,128)(2,1)S(1)} %pad_maximum_fusion.wpk, s32[8,128]{1,0:T(8,128)S(1)} %broadcast_in_dim.12.meta), custom_call_target="tpu_custom_call" | custom-call | flops 2013265920 | bytes 1048576 | tf_op jit(solution)/shard_map/pallas_call | solution.py:341
  75.7 0.7 fusion
  76.5 0.7 copy.14
  77.2 0.7 copy.18
  (3 shorter events, 0.0 us)
Async XLA Ops:
  1.9 0.7 copy-start.2
  1.9 0.8 %copy-start.3 = (s32[1,1,2,2]{3,2,1,0:T(2,128)S(1)}, s32[1,1,2,2]{3,2,1,0:T(2,128)}, u32[]{:S(2)}) copy-start(s32[1,1,2,2]{3,2,1,0:T(2,128)} %param.14) | copy-start | bytes 52
  1.9 2.8 %copy-start.1 = (bf16[128,384]{1,0:T(8,128)(2,1)S(1)}, bf16[128,384]{1,0:T(8,128)(2,1)}, u32[]{:S(2)}) copy-start(bf16[128,384]{1,0:T(8,128)(2,1)} %cot.1) | copy-start | bytes 294916
  2.6 2.2 %copy-start = (bf16[128,384]{1,0:T(8,128)(2,1)S(1)}, bf16[128,384]{1,0:T(8,128)(2,1)}, u32[]{:S(2)}) copy-start(bf16[128,384]{1,0:T(8,128)(2,1)} %tok.1) | copy-start | bytes 294916

commit v2 on v1

v2 whole, which is shorter than its diff:
```python
import functools
import math

import jax
import jax.numpy as jnp
from jax import lax
from jax.experimental import pallas as pl
from jax.experimental.pallas import tpu as pltpu
from jax.sharding import PartitionSpec as P

MESH = pl.DeviceIdType.MESH
F32 = jnp.float32
BF16 = jnp.bfloat16
NT = (((1,), (1,)), ((), ()))
NN = (((1,), (0,)), ((), ()))
TN = (((0,), (0,)), ((), ()))
NZ, NX, NY = 8, 4, 8
BLK = 64
DEAD = -64

FAMILIES = (
    ("right", 16), ("left", 16), ("pair", 16),
    ("table_z", 8), ("tile_z", 8), ("table_x", 24), ("tile_x", 24),
    ("part", 8), ("cr", 16), ("cl", 16), ("gx", 24), ("gz", 8),
)
BASE = {}
TOTAL = 0
for family, amount in FAMILIES:
    BASE[family] = TOTAL
    TOTAL += amount


def gelu_pair(hidden):
    inner = 0.7978845608028654 * (hidden + 0.044715 * hidden * hidden * hidden)
    tanh_term = jnp.tanh(inner)
    gelu_out = 0.5 * hidden * (1.0 + tanh_term)
    gelu_slope = 0.5 * (1.0 + tanh_term) + 0.5 * hidden * (
        1.0 - tanh_term * tanh_term
    ) * 0.7978845608028654 * (1.0 + 3.0 * 0.044715 * hidden * hidden)
    return (gelu_out, gelu_slope)


def place_in_order(row, y, core):
    dy = (row // 4 - y + NY) % NY
    other = jnp.where((row // 2) % 2 == core, 0, 1)
    near = jnp.minimum(dy, NY - dy)
    inner = 4 * near - 2 + 2 * other + jnp.where(dy > 4, 1, 0)
    return jnp.where(dy == 0, other, jnp.where(dy == 4, 14 + other, inner))


def kernel(
    tok, cot, w1, w2, coord1, count1, coord2, count2, ig, wg,
    w1v, w2v, c1, n1, c2, n2, xc, wall, mall, a1, a2, hid, ups, act, grd, part, psib, ssum, rbr, rbl,
    gr, xr, zs, zr, mv, dv, ms, md, send_sems, recv_sems, local_sems,
):
    row, col = lax.axis_index("row"), lax.axis_index("col")
    z, x, y, core = row // NX, row % NX, col // 2, col % 2

    def dev(dz=0, dx=0, dy=0, other=False):
        there = (1 - core) if other else core
        return ((z + dz) % NZ * NX + (x + dx) % NX, (y + dy) % NY * 2 + there)

    sibling = dev(other=True)
    right, left = dev(dy=1), dev(dy=NY - 1)
    z_right, z_left = dev(dz=1), dev(dz=NZ - 1)

    barrier = pltpu.get_barrier_semaphore()
    partners = [sibling, right, left]
    partners += [dev(dx=e) for e in range(1, NX)]
    partners += [dev(dz=e) for e in range(1, NZ)]
    for partner in partners:
        pl.semaphore_signal(barrier, inc=1, device_id=partner, device_id_type=MESH)

    loads = [
        pltpu.make_async_copy(src, dst, local_sems.at[n])
        for n, (src, dst) in enumerate((
            (w1, w1v), (w2, w2v), (coord1, c1), (count1, n1), (coord2, c2), (count2, n2),
            (tok, xc.at[col, 0]), (cot, xc.at[col, 1]),
        ))
    ]
    for load in loads:
        load.start()

    pending = []

    def describe(family, n, src, dst, target):
        slot = BASE[family] + n
        return pltpu.make_async_remote_copy(
            src_ref=src, dst_ref=dst, send_sem=send_sems.at[slot], recv_sem=recv_sems.at[slot],
            device_id=target, device_id_type=MESH,
        )

    def send(family, n, src, dst, target):
        copy = describe(family, n, src, dst, target)
        copy.start()
        pending.append(copy)

    def arrived(family, n, dst):
        describe(family, n, dst, dst, sibling).wait_recv()

    def shard(dy, other=False):
        return (y + dy) % NY * 2 + ((1 - core) if other else core)

    def plane(dz):
        return (z + dz) % NZ

    def piece(ref, j, h):
        return ref.at[j, pl.ds(64 * h, 64)]

    pl.semaphore_wait(barrier, len(partners))
    for j, own in ((0, tok), (1, cot)):
        for h in range(2):
            there = piece(xc.at[col], j, h)
            send("right", 2 * j + h, own.at[pl.ds(64 * h, 64)], there, right)
            send("left", 2 * j + h, own.at[pl.ds(64 * h, 64)], there, left)

    lane = lax.broadcasted_iota(jnp.int32, (1, 128), 1)
    low = lane < BLK
    for load in loads[:6]:
        load.wait()
    for k in range(2):
        wall[z, x, pl.ds(BLK * k, BLK), :] = jnp.concatenate(
            [w1v[k].astype(F32).T, w2v[k].astype(F32)], axis=1
        ).astype(BF16)
    hidden_places = [c1[0, 1], c1[1, 1], c2[0, 0], c2[1, 0]]
    model_places = [
        jnp.where(0 < n1[0, 0], c1[0, 0], DEAD), jnp.where(1 < n1[0, 0], c1[1, 0], DEAD),
        jnp.where(0 < n2[0, 0], c2[0, 1], DEAD), jnp.where(1 < n2[0, 0], c2[1, 1], DEAD),
    ]
    lane8 = lax.broadcasted_iota(jnp.int32, (8, 128), 1)
    line8 = lax.broadcasted_iota(jnp.int32, (8, 128), 0)
    meta = jnp.zeros((8, 128), jnp.int32)
    for n in range(4):
        meta = jnp.where((line8 == 0) & (lane8 == n), hidden_places[n], meta)
        meta = jnp.where(line8 == 1 + n, model_places[n], meta)
    mall[row] = meta

    def along_x(dz):
        there = plane(dz)
        for e in range(1, NX):
            at = mall.at[there * NX + x]
            send("table_x", 3 * dz + e - 1, at, at, dev(dx=e))
        for e in range(1, NX):
            at = wall.at[there, x]
            send("tile_x", 3 * dz + e - 1, at, at, dev(dx=e))

    for e in (1, 7, 2, 6, 3, 5, 4):
        send("table_z", e, mall.at[row], mall.at[row], dev(dz=e))
        send("tile_z", e, wall.at[z, x], wall.at[z, x], dev(dz=e))
    along_x(0)

    def planes_in(*away):
        for dz in away:
            arrived("table_z", NZ - dz, mall.at[plane(dz) * NX + x])
            arrived("tile_z", NZ - dz, wall.at[plane(dz), x])
            along_x(dz)

    def tables_in(*away):
        for dz in away:
            for e in range(1, NX):
                arrived("table_x", 3 * dz + e - 1, mall.at[plane(dz) * NX + (x + NX - e) % NX])

    def tiles_in(*away):
        for dz in away:
            for e in range(1, NX):
                arrived("tile_x", 3 * dz + e - 1, wall.at[plane(dz), (x + NX - e) % NX])

    hid[0] = jnp.zeros((BLK, 128), F32)
    ups[0] = jnp.zeros((BLK, 128), F32)
    for load in loads[6:]:
        load.wait()
    for j, own in ((0, tok), (1, cot)):
        send("pair", j, own, xc.at[col, j], sibling)

    def acts_in(d, j, h):
        n = 4 * (d - 1) + 2 * j + h
        if d <= 3 or j == 0:
            back = piece(xc.at[shard(NY - d)], j, h)
            arrived("right", n, back)
            if d < 3 or (d == 3 and j == 0):
                send("right", n + 4, back, back, right)
        if d <= 3 or j == 1:
            ahead = piece(xc.at[shard(d)], j, h)
            arrived("left", n, ahead)
            if d < 3 or (d == 3 and j == 1):
                send("left", n + 4, ahead, ahead, left)
        if h == 1:
            if d <= 3 or j == 0:
                whole = xc.at[shard(NY - d), j]
                send("pair", 2 * (NY - d) + j, whole, whole, sibling)
            if d <= 3 or j == 1:
                whole = xc.at[shard(d), j]
                send("pair", 2 * d + j, whole, whole, sibling)

    def places(c, matrix):
        found = []
        for i in range(2):
            for k in range(2):
                place = mall[2 * c + i, pl.ds(1 + 2 * matrix + k, 1), :] + 3 * i
                found.append([(jnp.where(low, 0, 1) + 2 * t) == place for t in range(3)])
        return found

    def build(c):
        ones, twos = places(c, 0), places(c, 1)
        for i in range(2):
            pack = wall[c // 2, (c % 2) * 2 + i].astype(F32)
            turned = pltpu.roll(pack, BLK, 1)
            first = jnp.where(low, pack, turned)
            second = jnp.where(low, turned, pack)
            for k in range(2):
                n = 2 * i + k
                here = slice(BLK * k, BLK * (k + 1))
                for t in range(3):
                    span = pl.ds(128 * t, 128)
                    a1[c, pl.ds(BLK * n, BLK), span] = jnp.where(ones[n][t], first[here], 0.0).astype(BF16)
                    a2[c, pl.ds(BLK * n, BLK), span] = jnp.where(twos[n][t], second[here], 0.0).astype(BF16)

    def build_planes(*away):
        for dz in away:
            there = plane(dz)

            def one_core(cc, carry, there=there):
                build(2 * there + cc)
                return carry

            lax.fori_loop(0, 2, one_core, 0)

    weights, sums = (a1, a2), (hid, ups)

    def forward_near(d, arrays, others):
        todo = []
        for other in others:
            for s, dy in enumerate(sorted({d, (NY - d) % NY})):
                place = {0: other, 4: 14 + other}.get(d, 4 * d - 2 + 2 * other + s)
                for j in arrays:
                    if other:
                        arrived("pair", 2 * dy + j, xc.at[shard(dy, True), j])
                    todo.append((j, shard(dy, other), place))
        for j, c, place in todo:
            product = lax.dot_general(weights[j][c], xc[c, j], NT, preferred_element_type=F32)
            sums[j][pl.ds(1 + 4 * place, 4)] = product.reshape(4, BLK, 128)
        for j, c, place in todo:
            for n in range(4):
                earlier = md[2 * c + n // 2, 2 * j + n % 2]
                at = 1 + 4 * place + n
                sums[j][at] = sums[j][at] + sums[j][earlier]

    def sort_slots():
        table = mall[:, 0, :]
        mv[...] = table
        rows = lax.broadcasted_iota(jnp.int32, (32, 128), 0)
        lanes = lax.broadcasted_iota(jnp.int32, (32, 128), 1)
        by_lane = 4 * place_in_order(lanes // 2, y, core) + lanes % 4
        by_row = 4 * place_in_order(rows, y, core) + 2 * (rows % 2)
        derived = jnp.zeros((32, 128), jnp.int32)
        for matrix, first in ((0, 0), (1, 2)):
            cols = [
                jnp.sum(jnp.where(lanes == first + k, table, 0), axis=1, keepdims=True) for k in range(2)
            ]
            flat = jnp.sum(
                jnp.where(rows == lanes // 2, jnp.where(lanes % 2 == 0, cols[0], cols[1]), 0),
                axis=0, keepdims=True,
            )
            for k in range(2):
                same = (flat == cols[k]) & (by_lane < by_row + k) & (lanes < 64)
                before = jnp.max(jnp.where(same, by_lane + 1, 0), axis=1, keepdims=True)
                derived = jnp.where(lanes == 2 * matrix + k, before, derived)
            ends = jnp.max(
                jnp.where((flat == rows) & (lanes < 64), by_lane + 1, 0), axis=1, keepdims=True
            )
            derived = jnp.where(lanes == 4 + matrix, ends, derived)
        dv[...] = derived
        copies = [
            pltpu.make_async_copy(mv, ms, local_sems.at[0]),
            pltpu.make_async_copy(dv, md, local_sems.at[1]),
        ]
        for copy in copies:
            copy.start()
        for copy in copies:
            copy.wait()

    planes_in(1, 7)
    acts_in(1, 0, 0)
    acts_in(1, 0, 1)
    planes_in(2, 6)
    acts_in(1, 1, 0)
    acts_in(1, 1, 1)
    planes_in(3, 5, 4)
    acts_in(2, 0, 0)
    tables_in(0, 1, 7)
    tiles_in(0, 1, 7)
    build_planes(0, 1, 7)
    acts_in(2, 0, 1)
    acts_in(2, 1, 0)
    tables_in(2, 6)
    tiles_in(2, 6)
    build_planes(2, 6)
    acts_in(2, 1, 1)
    tables_in(3, 5, 4)
    sort_slots()
    acts_in(3, 0, 0)
    tiles_in(3, 5, 4)
    build_planes(3, 5, 4)
    acts_in(3, 0, 1)
    forward_near(0, (0, 1), (0, 1))
    forward_near(1, (0,), (0, 1))
    acts_in(3, 1, 0)
    forward_near(1, (1,), (0, 1))
    acts_in(3, 1, 1)
    forward_near(2, (0,), (0, 1))
    forward_near(2, (1,), (0, 1))
    acts_in(4, 0, 0)
    acts_in(4, 1, 0)
    forward_near(3, (0,), (0, 1))
    acts_in(4, 0, 1)
    acts_in(4, 1, 1)
    forward_near(3, (1,), (0, 1))
    forward_near(4, (0, 1), (0,))
    forward_near(4, (0, 1), (1,))

    def middle(q, carry):
        gelu_out, gelu_slope = gelu_pair(hid[md[q, 4]])
        act[q] = gelu_out.astype(BF16)
        grd[q] = (ups[md[q, 5]] * gelu_slope).astype(BF16)
        return carry

    lax.fori_loop(0, 24, middle, 0)

    def pick(product, found):
        total = jnp.where(found[0], product[:, 0:128], 0.0)
        for t in range(1, 3):
            total = total + jnp.where(found[t], product[:, 128 * t : 128 * (t + 1)], 0.0)
        return total + pltpu.roll(total, BLK, 1)

    def chosen(source, c, first):
        return jnp.concatenate([source[ms[2 * c + n // 2, first + n % 2]] for n in range(4)], axis=0)

    def to_input(c):
        part[c] = lax.dot_general(
            chosen(grd, c, 0), a1[c], TN, preferred_element_type=F32
        ).astype(BF16)

    def to_blocks(c):
        ones, twos = places(c, 0), places(c, 1)
        one = lax.dot_general(chosen(grd, c, 0), xc[c, 0], NN, preferred_element_type=F32)
        two = lax.dot_general(chosen(act, c, 2), xc[c, 1], NN, preferred_element_type=F32)
        for n in range(4):
            span = slice(BLK * n, BLK * (n + 1))
            both = jnp.where(low, pick(one[span], ones[n]), pick(two[span], twos[n]))
            gr[c // 2, (c % 2) * 2 + n // 2, pl.ds(BLK * (n % 2), BLK), :] = both.astype(BF16)

    def quarter(ref, q):
        return ref.at[pl.ds(32 * q, 32)]

    def settle(dy, *quarters):
        there = (y + dy) % NY
        for q in quarters:
            rows = pl.ds(32 * q, 32)
            total = part[shard(dy), rows].astype(F32) + psib[there, rows].astype(F32)
            if dy == 0:
                for family, buffer in (("cr", rbr), ("cl", rbl)):
                    arrived(family, 12 + q, quarter(buffer.at[3], q))
                    total = total + buffer[3, rows].astype(F32)
                ig[rows, :] = total
                continue
            chain, step = (0, 4 - dy) if dy < 4 else (1, dy - 4)
            if dy == 4:
                chain = q // 2
            family, buffer, target = (("cr", rbr, right), ("cl", rbl, left))[chain]
            if step > 1 or (step == 1 and q // 2 == chain):
                arrived(family, 4 * step - 4 + q, quarter(buffer.at[step - 1], q))
                total = total + buffer[step - 1, rows].astype(F32)
            ssum[there, rows] = total.astype(BF16)
            send(family, 4 * step + q, quarter(ssum.at[there], q), quarter(buffer.at[step], q), target)

    def paired(*away):
        for dy in away:
            arrived("part", dy, psib.at[(y + dy) % NY])

    def plane_sum(dz):
        total = gr[plane(dz), x].astype(F32)
        for e in range(1, NX):
            arrived("gx", dz * 3 + e - 1, xr.at[dz, e - 1])
            total = total + xr[dz, e - 1].astype(F32)
        return total

    def plane_on(*away):
        for dz in away:
            zs[dz] = plane_sum(dz).astype(BF16)
            send("gz", dz, zs.at[dz], zr.at[dz], dev(dz=dz))

    def inputs_step(dy):
        there = (y + dy) % NY
        for other in (True, False):
            to_input(shard(dy, other))
            if other:
                send("part", dy, part.at[shard(dy, True)], psib.at[there], sibling)

    def blocks_step(dz):
        there = plane(dz)
        for cc in range(2):
            to_blocks(there * 2 + cc)
        for e in range(1, NX):
            send("gx", dz * 3 + e - 1, gr.at[there, (x + e) % NX], xr.at[dz, e - 1], dev(dx=e))

    inputs_step(4)
    inputs_step(3)
    inputs_step(5)
    blocks_step(4)
    paired(4)
    settle(4, 0, 2, 1, 3)
    paired(3, 5)
    settle(3, 2, 3)
    settle(5, 0, 1)
    inputs_step(2)
    blocks_step(3)
    inputs_step(6)
    blocks_step(5)
    for n in range(2):
        settle(3, n)
        settle(5, 2 + n)
    paired(2, 6)
    for n in range(2):
        settle(2, 2 + n)
        settle(6, n)
    inputs_step(1)
    blocks_step(2)
    plane_on(4)
    for n in range(2):
        settle(2, n)
        settle(6, 2 + n)
    inputs_step(7)
    blocks_step(6)
    plane_on(3)
    paired(1, 7)
    for n in range(2):
        settle(1, 2 + n)
        settle(7, n)
    inputs_step(0)
    blocks_step(1)
    plane_on(5)
    for n in range(2):
        settle(1, n)
        settle(7, 2 + n)
    blocks_step(7)
    plane_on(2)
    blocks_step(0)
    plane_on(6)
    paired(0)
    plane_on(1, 7)
    settle(0, 2, 3, 0, 1)
    total = plane_sum(0)
    for e in range(1, NZ):
        arrived("gz", e, zr.at[e])
        total = total + zr[e].astype(F32)
    wg[...] = total

    for copy in pending:
        copy.wait_send()


def finish(scale, ig, wg, input_grad, grad_one, grad_two, one, two, sems):
    copies = [pltpu.make_async_copy(ig, input_grad, sems.at[0])]
    copies[0].start()
    for k in range(2):
        rows = pl.ds(BLK * k, BLK)
        one[k] = wg[rows, 0:BLK].T * scale
        two[k] = wg[rows, BLK : 2 * BLK] * scale
    copies.append(pltpu.make_async_copy(one, grad_one, sems.at[1]))
    copies.append(pltpu.make_async_copy(two, grad_two, sems.at[2]))
    for copy in copies[1:]:
        copy.start()
    for copy in copies:
        copy.wait()


def shards(tokens, cotangent, w1_blocks, w1_coords, w1_count, w2_blocks, w2_coords, w2_count):
    scale = 1.0 / math.sqrt(4096)
    shard = (128, 384)
    blocks = (2, BLK, BLK)
    vmem = pl.BlockSpec(memory_space=pltpu.VMEM)
    anywhere = pl.BlockSpec(memory_space=pl.ANY)
    ig, wg = pl.pallas_call(
        kernel,
        out_shape=(
            jax.ShapeDtypeStruct(shard, F32),
            jax.ShapeDtypeStruct((128, 128), F32),
        ),
        in_specs=[anywhere] * 8,
        out_specs=(vmem, vmem),
        scratch_shapes=[
            pltpu.VMEM(blocks, BF16),
            pltpu.VMEM(blocks, BF16),
            pltpu.SMEM((2, 2), jnp.int32),
            pltpu.SMEM((1, 1), jnp.int32),
            pltpu.SMEM((2, 2), jnp.int32),
            pltpu.SMEM((1, 1), jnp.int32),
            pltpu.VMEM((16, 2) + shard, BF16),
            pltpu.VMEM((NZ, NX, 128, 128), BF16),
            pltpu.VMEM((32, 8, 128), jnp.int32),
            pltpu.VMEM((16, 256, 384), BF16),
            pltpu.VMEM((16, 256, 384), BF16),
            pltpu.VMEM((65, BLK, 128), F32),
            pltpu.VMEM((65, BLK, 128), F32),
            pltpu.VMEM((24, BLK, 128), BF16),
            pltpu.VMEM((24, BLK, 128), BF16),
            pltpu.VMEM((16,) + shard, BF16),
            pltpu.VMEM((8,) + shard, BF16),
            pltpu.VMEM((8,) + shard, BF16),
            pltpu.VMEM((4,) + shard, BF16),
            pltpu.VMEM((4,) + shard, BF16),
            pltpu.VMEM((NZ, NX, 128, 128), BF16),
            pltpu.VMEM((NZ, 3, 128, 128), BF16),
            pltpu.VMEM((NZ, 128, 128), BF16),
            pltpu.VMEM((NZ, 128, 128), BF16),
            pltpu.VMEM((32, 128), jnp.int32),
            pltpu.VMEM((32, 128), jnp.int32),
            pltpu.SMEM((32, 128), jnp.int32),
            pltpu.SMEM((32, 128), jnp.int32),
            pltpu.SemaphoreType.DMA((TOTAL,)),
            pltpu.SemaphoreType.DMA((TOTAL,)),
            pltpu.SemaphoreType.DMA((8,)),
        ],
        compiler_params=pltpu.CompilerParams(
            collective_id=0, has_side_effects=True, vmem_limit_bytes=56 * 1024 * 1024
        ),
        cost_estimate=pl.CostEstimate(
            flops=16 * 5 * 2 * 256 * 384 * 128, bytes_accessed=1 << 20, transcendentals=24 * 64 * 128
        ),
    )(
        tokens, cotangent, w1_blocks.reshape(blocks), w2_blocks.reshape(blocks),
        w1_coords.reshape(2, 2), w1_count, w2_coords.reshape(2, 2), w2_count,
    )
    input_grad, grad_one, grad_two = pl.pallas_call(
        functools.partial(finish, scale),
        out_shape=(
            jax.ShapeDtypeStruct(shard, F32),
            jax.ShapeDtypeStruct(blocks, F32),
            jax.ShapeDtypeStruct(blocks, F32),
        ),
        in_specs=[vmem] * 2,
        out_specs=(anywhere,) * 3,
        scratch_shapes=[
            pltpu.VMEM(blocks, F32), pltpu.VMEM(blocks, F32), pltpu.SemaphoreType.DMA((3,)),
        ],
    )(ig, wg)
    return (input_grad, grad_one.reshape(w1_blocks.shape), grad_two.reshape(w2_blocks.shape))


def solution(mesh):
    wide = P("row", "col", None, None, None)
    return jax.shard_map(
        shards,
        mesh=mesh,
        in_specs=(
            P("row", "col"), P("row", "col"),
            wide, P("row", "col", None, None), P("row", "col"),
            wide, P("row", "col", None, None), P("row", "col"),
        ),
        out_specs=(P("row", "col"), wide, wide),
        check_vma=False,
    )
```

time: 78.1 us -> 65.1 us (0.83)
  the two profiles are of different devices: /device:TPU:4 before, /device:TPU:24 now
where the time goes in v2:
time: 65.1 us; the launch traced here: 65 us
  Pallas kernels  63 us (97%)
  between operations  1.93 us (3%)
    pallas_call x1, Pallas kernels, shards(): pl.pallas_call(kernel, out_shape=(jax.ShapeDtypeStruct(shard, F32), jax.S...  61.3 us
    pallas_call x1, Pallas kernels, shards(): pl.pallas_call(functools.partial(finish, scale), out_shape=(jax.ShapeDtyp...  1.75 us

profile of v2, /device:TPU:24, one launch (start us, length us, event | category | flops | bytes accessed | tf_op | source)
XLA Modules:
  0.0 65.0 jit_solution(5988545379003115540)
XLA Ops:
  1.9 61.3 %shard_map.103 = (f32[128,384]{1,0:T(8,128)}, f32[128,128]{1,0:T(8,128)}) custom-call(bf16[128,384]{1,0:T(8,128)(2,1)} %tok.1, bf16[128,384]{1,0:T(8,128)(2,1)} %cot.1, bf16[2,64,64]{2,1,0:T(8,128)(2,1)} %bitcast.8, bf16[2,64,64]{2,1,0:T(8,128)(2,1)} %bitcast.9, s32[2,2]{1,0:T(2,128)} %bitcast.10, s32[1,1]{1,0:T(1,128)S(6)} %copy.11.count1, ...), custom_call_target="tpu_custom_call" | custom-call | flops 2013265920 | bytes 1048576 | tf_op jit(solution)/shard_map/pallas_call | solution.py:483
  63.2 1.7 %shard_map.104 = (f32[128,384]{1,0:T(8,128)}, f32[2,64,64]{2,1,0:T(8,128)}, f32[2,64,64]{2,1,0:T(8,128)}) custom-call(f32[128,384]{1,0:T(8,128)} %get-tuple-element.8.ig, f32[128,128]{1,0:T(8,128)} %get-tuple-element.9.wg), custom_call_target="tpu_custom_call" | custom-call | tf_op jit(solution)/shard_map/pallas_call | solution.py:534

commit v3 on v2

--- a/solution.py
+++ b/solution.py
@@ -49,9 +49,9 @@
 
 
 def kernel(
-    tok, cot, w1, w2, coord1, count1, coord2, count2, ig, wg,
+    scale, tok, cot, w1, w2, coord1, count1, coord2, count2, ig, g1, g2,
     w1v, w2v, c1, n1, c2, n2, xc, wall, mall, a1, a2, hid, ups, act, grd, part, psib, ssum, rbr, rbl,
-    gr, xr, zs, zr, mv, dv, ms, md, send_sems, recv_sems, local_sems,
+    igv, g1v, g2v, gr, xr, zs, zr, mv, dv, ms, md, send_sems, recv_sems, local_sems,
 ):
     row, col = lax.axis_index("row"), lax.axis_index("col")
     z, x, y, core = row // NX, row % NX, col // 2, col % 2
@@ -361,7 +361,8 @@
                 for family, buffer in (("cr", rbr), ("cl", rbl)):
                     arrived(family, 12 + q, quarter(buffer.at[3], q))
                     total = total + buffer[3, rows].astype(F32)
-                ig[rows, :] = total
+                igv[rows, :] = total
+                pltpu.make_async_copy(quarter(igv, q), quarter(ig, q), local_sems.at[q]).start()
                 continue
             chain, step = (0, 4 - dy) if dy < 4 else (1, dy - 4)
             if dy == 4:
@@ -404,71 +405,82 @@
             send("gx", dz * 3 + e - 1, gr.at[there, (x + e) % NX], xr.at[dz, e - 1], dev(dx=e))
 
     inputs_step(4)
+    blocks_step(4)
     inputs_step(3)
     inputs_step(5)
-    blocks_step(4)
+    blocks_step(3)
+    blocks_step(5)
+    inputs_step(2)
+    inputs_step(6)
     paired(4)
     settle(4, 0, 2, 1, 3)
+    blocks_step(2)
     paired(3, 5)
     settle(3, 2, 3)
     settle(5, 0, 1)
-    inputs_step(2)
-    blocks_step(3)
-    inputs_step(6)
-    blocks_step(5)
+    blocks_step(6)
+    inputs_step(1)
+    inputs_step(7)
+    blocks_step(1)
+    blocks_step(7)
+    inputs_step(0)
+    blocks_step(0)
+    plane_on(4)
     for n in range(2):
         settle(3, n)
         settle(5, 2 + n)
+    plane_on(3)
     paired(2, 6)
     for n in range(2):
         settle(2, 2 + n)
         settle(6, n)
-    inputs_step(1)
-    blocks_step(2)
-    plane_on(4)
+    plane_on(5)
     for n in range(2):
         settle(2, n)
         settle(6, 2 + n)
-    inputs_step(7)
-    blocks_step(6)
-    plane_on(3)
+    plane_on(2)
     paired(1, 7)
     for n in range(2):
         settle(1, 2 + n)
         settle(7, n)
-    inputs_step(0)
-    blocks_step(1)
-    plane_on(5)
+    plane_on(6)
     for n in range(2):
         settle(1, n)
         settle(7, 2 + n)
-    blocks_step(7)
-    plane_on(2)
-    blocks_step(0)
-    plane_on(6)
+    plane_on(1)
+    plane_on(7)
     paired(0)
-    plane_on(1, 7)
     settle(0, 2, 3, 0, 1)
     total = plane_sum(0)
     for e in range(1, NZ):
         arrived("gz", e, zr.at[e])
         total = total + zr[e].astype(F32)
-    wg[...] = total
+    total = total * scale
+    for k in range(2):
+        here = slice(BLK * k, BLK * (k + 1))
+        g1v[k] = total[here, 0:BLK].T
+        g2v[k] = total[here, BLK:128]
+    stores = [
+        pltpu.make_async_copy(g1v, g1, local_sems.at[4]),
+        pltpu.make_async_copy(g2v, g2, local_sems.at[5]),
+    ]
+    for store in stores:
+        store.start()
+    for q in range(4):
+        pltpu.make_async_copy(quarter(igv, q), quarter(ig, q), local_sems.at[q]).wait()
+    for store in stores:
+        store.wait()
 
     for copy in pending:
         copy.wait_send()
 
 
-def finish(scale, ig, wg, input_grad, grad_one, grad_two, one, two, sems):
-    copies = [pltpu.make_async_copy(ig, input_grad, sems.at[0])]
-    copies[0].start()
-    for k in range(2):
-        rows = pl.ds(BLK * k, BLK)
-        one[k] = wg[rows, 0:BLK].T * scale
-        two[k] = wg[rows, BLK : 2 * BLK] * scale
-    copies.append(pltpu.make_async_copy(one, grad_one, sems.at[1]))
-    copies.append(pltpu.make_async_copy(two, grad_two, sems.at[2]))
-    for copy in copies[1:]:
+def finish(ig, g1, g2, input_grad, grad_one, grad_two, sems):
+    copies = [
+        pltpu.make_async_copy(src, dst, sems.at[n])
+        for n, (src, dst) in enumerate(((ig, input_grad), (g1, grad_one), (g2, grad_two)))
+    ]
+    for copy in copies:
         copy.start()
     for copy in copies:
         copy.wait()
@@ -478,16 +490,17 @@
     scale = 1.0 / math.sqrt(4096)
     shard = (128, 384)
     blocks = (2, BLK, BLK)
-    vmem = pl.BlockSpec(memory_space=pltpu.VMEM)
     anywhere = pl.BlockSpec(memory_space=pl.ANY)
-    ig, wg = pl.pallas_call(
-        kernel,
-        out_shape=(
-            jax.ShapeDtypeStruct(shard, F32),
-            jax.ShapeDtypeStruct((128, 128), F32),
-        ),
+    results = (
+        jax.ShapeDtypeStruct(shard, F32),
+        jax.ShapeDtypeStruct(blocks, F32),
+        jax.ShapeDtypeStruct(blocks, F32),
+    )
+    halfway = pl.pallas_call(
+        functools.partial(kernel, scale),
+        out_shape=results,
         in_specs=[anywhere] * 8,
-        out_specs=(vmem, vmem),
+        out_specs=(anywhere,) * 3,
         scratch_shapes=[
             pltpu.VMEM(blocks, BF16),
             pltpu.VMEM(blocks, BF16),
@@ -509,6 +522,9 @@
             pltpu.VMEM((8,) + shard, BF16),
             pltpu.VMEM((4,) + shard, BF16),
             pltpu.VMEM((4,) + shard, BF16),
+            pltpu.VMEM(shard, F32),
+            pltpu.VMEM(blocks, F32),
+            pltpu.VMEM(blocks, F32),
             pltpu.VMEM((NZ, NX, 128, 128), BF16),
             pltpu.VMEM((NZ, 3, 128, 128), BF16),
             pltpu.VMEM((NZ, 128, 128), BF16),
@@ -532,18 +548,12 @@
         w1_coords.reshape(2, 2), w1_count, w2_coords.reshape(2, 2), w2_count,
     )
     input_grad, grad_one, grad_two = pl.pallas_call(
-        functools.partial(finish, scale),
-        out_shape=(
-            jax.ShapeDtypeStruct(shard, F32),
-            jax.ShapeDtypeStruct(blocks, F32),
-            jax.ShapeDtypeStruct(blocks, F32),
-        ),
-        in_specs=[vmem] * 2,
+        finish,
+        out_shape=results,
+        in_specs=[pl.BlockSpec(memory_space=pltpu.VMEM)] * 3,
         out_specs=(anywhere,) * 3,
-        scratch_shapes=[
-            pltpu.VMEM(blocks, F32), pltpu.VMEM(blocks, F32), pltpu.SemaphoreType.DMA((3,)),
-        ],
-    )(ig, wg)
+        scratch_shapes=[pltpu.SemaphoreType.DMA((3,))],
+    )(*halfway)
     return (input_grad, grad_one.reshape(w1_blocks.shape), grad_two.reshape(w2_blocks.shape))
 
 

time: 65.1 us -> 62.1 us (0.954)
  the two profiles are of different devices: /device:TPU:24 before, /device:TPU:16 now
where the time goes in v3:
time: 62.1 us; the launch traced here: 61.9 us
  Pallas kernels  60 us (97%)
  between operations  1.93 us (3%)
    pallas_call x1, Pallas kernels, shards(): pl.pallas_call(functools.partial(kernel, scale), out_shape=results, in_sp...  58.3 us
    pallas_call x1, Pallas kernels, shards(): pl.pallas_call(finish, out_shape=results, in_specs=[pl.BlockSpec(memory_s...  1.71 us

profile of v3, /device:TPU:16, one launch (start us, length us, event | category | flops | bytes accessed | tf_op | source)
XLA Modules:
  0.0 61.9 jit_solution(14896178838668279210)
XLA Ops:
  1.9 58.3 %shard_map.103 = (f32[128,384]{1,0:T(8,128)}, f32[2,64,64]{2,1,0:T(8,128)}, f32[2,64,64]{2,1,0:T(8,128)}) custom-call(bf16[128,384]{1,0:T(8,128)(2,1)} %tok.1, bf16[128,384]{1,0:T(8,128)(2,1)} %cot.1, bf16[2,64,64]{2,1,0:T(8,128)(2,1)} %bitcast.8, bf16[2,64,64]{2,1,0:T(8,128)(2,1)} %bitcast.9, s32[2,2]{1,0:T(2,128)} %bitcast.10, s32[1,1]{1,0:T(1,128)S(6)} %copy.11.count1, ...), custom_call_target="tpu_custom_call" | custom-call | flops 2013265920 | bytes 1048576 | tf_op jit(solution)/shard_map/pallas_call | solution.py:499
  60.2 1.7 %shard_map.104 = (f32[128,384]{1,0:T(8,128)}, f32[2,64,64]{2,1,0:T(8,128)}, f32[2,64,64]{2,1,0:T(8,128)}) custom-call(f32[128,384]{1,0:T(8,128)} %get-tuple-element.9.ig, f32[2,64,64]{2,1,0:T(8,128)} %get-tuple-element.10.g1, f32[2,64,64]{2,1,0:T(8,128)} %get-tuple-element.11.g2), custom_call_target="tpu_custom_call" | custom-call | tf_op jit(solution)/shard_map/pallas_call | solution.py:550

commit v4 on v3

--- a/solution.py
+++ b/solution.py
@@ -21,7 +21,7 @@
 FAMILIES = (
     ("right", 16), ("left", 16), ("pair", 16),
     ("table_z", 8), ("tile_z", 8), ("table_x", 24), ("tile_x", 24),
-    ("part", 8), ("cr", 16), ("cl", 16), ("gx", 24), ("gz", 8),
+    ("part", 8), ("cr", 16), ("cl", 16), ("crx", 4), ("clx", 4), ("gx", 24), ("gz", 8),
 )
 BASE = {}
 TOTAL = 0
@@ -50,8 +50,8 @@
 
 def kernel(
     scale, tok, cot, w1, w2, coord1, count1, coord2, count2, ig, g1, g2,
-    w1v, w2v, c1, n1, c2, n2, xc, wall, mall, a1, a2, hid, ups, act, grd, part, psib, ssum, rbr, rbl,
-    igv, g1v, g2v, gr, xr, zs, zr, mv, dv, ms, md, send_sems, recv_sems, local_sems,
+    w1v, w2v, c1, n1, c2, n2, xc, wall, mall, a1, a2, hid, ups, act, grd, part, psib, ssum, rbr, rbl, rbx,
+    gr, xr, zs, zr, mv, dv, ms, md, send_sems, recv_sems, local_sems,
 ):
     row, col = lax.axis_index("row"), lax.axis_index("col")
     z, x, y, core = row // NX, row % NX, col // 2, col % 2
@@ -65,7 +65,8 @@
     z_right, z_left = dev(dz=1), dev(dz=NZ - 1)
 
     barrier = pltpu.get_barrier_semaphore()
-    partners = [sibling, right, left]
+    right_other, left_other = dev(dy=1, other=True), dev(dy=NY - 1, other=True)
+    partners = [sibling, right, left, right_other, left_other]
     partners += [dev(dx=e) for e in range(1, NX)]
     partners += [dev(dz=e) for e in range(1, NZ)]
     for partner in partners:
@@ -285,35 +286,36 @@
     planes_in(2, 6)
     acts_in(1, 1, 0)
     acts_in(1, 1, 1)
-    planes_in(3, 5, 4)
     acts_in(2, 0, 0)
+    planes_in(3, 5)
+    acts_in(2, 0, 1)
+    planes_in(4)
     tables_in(0, 1, 7)
     tiles_in(0, 1, 7)
     build_planes(0, 1, 7)
-    acts_in(2, 0, 1)
     acts_in(2, 1, 0)
+    acts_in(2, 1, 1)
     tables_in(2, 6)
     tiles_in(2, 6)
     build_planes(2, 6)
-    acts_in(2, 1, 1)
+    acts_in(3, 0, 0)
     tables_in(3, 5, 4)
     sort_slots()
-    acts_in(3, 0, 0)
+    acts_in(3, 0, 1)
+    acts_in(3, 1, 0)
     tiles_in(3, 5, 4)
     build_planes(3, 5, 4)
-    acts_in(3, 0, 1)
+    acts_in(3, 1, 1)
     forward_near(0, (0, 1), (0, 1))
     forward_near(1, (0,), (0, 1))
-    acts_in(3, 1, 0)
     forward_near(1, (1,), (0, 1))
-    acts_in(3, 1, 1)
+    acts_in(4, 0, 0)
+    acts_in(4, 1, 0)
     forward_near(2, (0,), (0, 1))
     forward_near(2, (1,), (0, 1))
-    acts_in(4, 0, 0)
-    acts_in(4, 1, 0)
-    forward_near(3, (0,), (0, 1))
     acts_in(4, 0, 1)
     acts_in(4, 1, 1)
+    forward_near(3, (0,), (0, 1))
     forward_near(3, (1,), (0, 1))
     forward_near(4, (0, 1), (0,))
     forward_near(4, (0, 1), (1,))
@@ -361,18 +363,26 @@
                 for family, buffer in (("cr", rbr), ("cl", rbl)):
                     arrived(family, 12 + q, quarter(buffer.at[3], q))
                     total = total + buffer[3, rows].astype(F32)
-                igv[rows, :] = total
-                pltpu.make_async_copy(quarter(igv, q), quarter(ig, q), local_sems.at[q]).start()
+                ig[rows, :] = total
                 continue
             chain, step = (0, 4 - dy) if dy < 4 else (1, dy - 4)
-            if dy == 4:
-                chain = q // 2
             family, buffer, target = (("cr", rbr, right), ("cl", rbl, left))[chain]
-            if step > 1 or (step == 1 and q // 2 == chain):
+            if step > 1 or q // 2 == chain:
                 arrived(family, 4 * step - 4 + q, quarter(buffer.at[step - 1], q))
                 total = total + buffer[step - 1, rows].astype(F32)
+            if step == 1 and q // 2 == chain:
+                arrived(family + "x", q, quarter(rbx, q))
+                total = total + rbx[rows].astype(F32)
             ssum[there, rows] = total.astype(BF16)
             send(family, 4 * step + q, quarter(ssum.at[there], q), quarter(buffer.at[step], q), target)
+
+    def opening():
+        for q in (0, 2, 1, 3):
+            family, buffer, target, target_other = (
+                ("cr", rbr, right, right_other), ("cl", rbl, left, left_other)
+            )[q // 2]
+            send(family, q, quarter(part.at[shard(4)], q), quarter(buffer.at[0], q), target)
+            send(family + "x", q, quarter(part.at[shard(4, True)], q), quarter(rbx, q), target_other)
 
     def paired(*away):
         for dy in away:
@@ -394,7 +404,7 @@
         there = (y + dy) % NY
         for other in (True, False):
             to_input(shard(dy, other))
-            if other:
+            if other and dy != 4:
                 send("part", dy, part.at[shard(dy, True)], psib.at[there], sibling)
 
     def blocks_step(dz):
@@ -405,6 +415,7 @@
             send("gx", dz * 3 + e - 1, gr.at[there, (x + e) % NX], xr.at[dz, e - 1], dev(dx=e))
 
     inputs_step(4)
+    opening()
     blocks_step(4)
     inputs_step(3)
     inputs_step(5)
@@ -412,8 +423,6 @@
     blocks_step(5)
     inputs_step(2)
     inputs_step(6)
-    paired(4)
-    settle(4, 0, 2, 1, 3)
     blocks_step(2)
     paired(3, 5)
     settle(3, 2, 3)
@@ -458,18 +467,8 @@
     total = total * scale
     for k in range(2):
         here = slice(BLK * k, BLK * (k + 1))
-        g1v[k] = total[here, 0:BLK].T
-        g2v[k] = total[here, BLK:128]
-    stores = [
-        pltpu.make_async_copy(g1v, g1, local_sems.at[4]),
-        pltpu.make_async_copy(g2v, g2, local_sems.at[5]),
-    ]
-    for store in stores:
-        store.start()
-    for q in range(4):
-        pltpu.make_async_copy(quarter(igv, q), quarter(ig, q), local_sems.at[q]).wait()
-    for store in stores:
-        store.wait()
+        g1[k] = total[here, 0:BLK].T
+        g2[k] = total[here, BLK:128]
 
     for copy in pending:
         copy.wait_send()
@@ -496,11 +495,19 @@
         jax.ShapeDtypeStruct(blocks, F32),
         jax.ShapeDtypeStruct(blocks, F32),
     )
+    vmem = pl.BlockSpec(memory_space=pltpu.VMEM)
+    tokens, cotangent, w1_in, w2_in, c1_in, c2_in = [
+        pltpu.with_memory_space_constraint(array, pltpu.HBM)
+        for array in (
+            tokens, cotangent, w1_blocks.reshape(blocks), w2_blocks.reshape(blocks),
+            w1_coords.reshape(2, 2), w2_coords.reshape(2, 2),
+        )
+    ]
     halfway = pl.pallas_call(
         functools.partial(kernel, scale),
-        out_shape=results,
+        out_shape=tuple(pltpu.VMEM(result.shape, F32) for result in results),
         in_specs=[anywhere] * 8,
-        out_specs=(anywhere,) * 3,
+        out_specs=(vmem,) * 3,
         scratch_shapes=[
             pltpu.VMEM(blocks, BF16),
             pltpu.VMEM(blocks, BF16),
@@ -522,9 +529,7 @@
             pltpu.VMEM((8,) + shard, BF16),
             pltpu.VMEM((4,) + shard, BF16),
             pltpu.VMEM((4,) + shard, BF16),
-            pltpu.VMEM(shard, F32),
-            pltpu.VMEM(blocks, F32),
-            pltpu.VMEM(blocks, F32),
+            pltpu.VMEM(shard, BF16),
             pltpu.VMEM((NZ, NX, 128, 128), BF16),
             pltpu.VMEM((NZ, 3, 128, 128), BF16),
             pltpu.VMEM((NZ, 128, 128), BF16),
@@ -538,22 +543,19 @@
             pltpu.SemaphoreType.DMA((8,)),
         ],
         compiler_params=pltpu.CompilerParams(
-            collective_id=0, has_side_effects=True, vmem_limit_bytes=56 * 1024 * 1024
+            collective_id=0, has_side_effects=True, vmem_limit_bytes=48 * 1024 * 1024
         ),
         cost_estimate=pl.CostEstimate(
             flops=16 * 5 * 2 * 256 * 384 * 128, bytes_accessed=1 << 20, transcendentals=24 * 64 * 128
         ),
-    )(
-        tokens, cotangent, w1_blocks.reshape(blocks), w2_blocks.reshape(blocks),
-        w1_coords.reshape(2, 2), w1_count, w2_coords.reshape(2, 2), w2_count,
-    )
+    )(tokens, cotangent, w1_in, w2_in, c1_in, w1_count, c2_in, w2_count)
     input_grad, grad_one, grad_two = pl.pallas_call(
         finish,
         out_shape=results,
-        in_specs=[pl.BlockSpec(memory_space=pltpu.VMEM)] * 3,
+        in_specs=[vmem] * 3,
         out_specs=(anywhere,) * 3,
         scratch_shapes=[pltpu.SemaphoreType.DMA((3,))],
-    )(*halfway)
+    )(*[pltpu.with_memory_space_constraint(array, pltpu.VMEM) for array in halfway])
     return (input_grad, grad_one.reshape(w1_blocks.shape), grad_two.reshape(w2_blocks.shape))
 
 

time: 62.1 us -> 60 us (0.966)
  the two profiles are of different devices: /device:TPU:16 before, /device:TPU:24 now
where the time goes in v4:
time: 60 us; the launch traced here: 59.8 us
  Pallas kernels  57.9 us (96%)
  between operations  1.93 us (3%)
    pallas_call x1, Pallas kernels, shards(): pl.pallas_call(functools.partial(kernel, scale), out_shape=tuple((pltpu.V...  57.2 us

profile of v4, /device:TPU:24, one launch (start us, length us, event | category | flops | bytes accessed | tf_op | source)
XLA Modules:
  0.0 59.8 jit_solution(15836513689164879612)
XLA Ops:
  1.9 57.2 %shard_map.103 = (f32[128,384]{1,0:T(8,128)S(1)}, f32[2,64,64]{2,1,0:T(8,128)S(1)}, f32[2,64,64]{2,1,0:T(8,128)S(1)}) custom-call(bf16[128,384]{1,0:T(8,128)(2,1)} %tok.1, bf16[128,384]{1,0:T(8,128)(2,1)} %cot.1, bf16[2,64,64]{2,1,0:T(8,128)(2,1)} %bitcast.8, bf16[2,64,64]{2,1,0:T(8,128)(2,1)} %bitcast.9, s32[2,2]{1,0:T(2,128)} %bitcast.10, ...), custom_call_target="tpu_custom_call" | custom-call | flops 2013265920 | bytes 1048576 | tf_op jit(solution)/shard_map/pallas_call | solution.py:506
  59.1 0.7 %shard_map.104 = (f32[128,384]{1,0:T(8,128)}, f32[2,64,64]{2,1,0:T(8,128)}, f32[2,64,64]{2,1,0:T(8,128)}) custom-call(f32[128,384]{1,0:T(8,128)S(1)} %get-tuple-element.9.ig, f32[2,64,64]{2,1,0:T(8,128)S(1)} %get-tuple-element.10.g1, f32[2,64,64]{2,1,0:T(8,128)S(1)} %get-tuple-element.11.g2), custom_call_target="tpu_custom_call" | custom-call | tf_op jit(solution)/shard_map/pallas_call | solution.py:552

commit v5 on v4

--- a/solution.py
+++ b/solution.py
@@ -420,9 +420,9 @@
     inputs_step(3)
     inputs_step(5)
     blocks_step(3)
-    blocks_step(5)
     inputs_step(2)
     inputs_step(6)
+    blocks_step(5)
     blocks_step(2)
     paired(3, 5)
     settle(3, 2, 3)
@@ -431,35 +431,35 @@
     inputs_step(1)
     inputs_step(7)
     blocks_step(1)
+    for n in range(2):
+        settle(3, n)
+        settle(5, 2 + n)
     blocks_step(7)
     inputs_step(0)
     blocks_step(0)
     plane_on(4)
-    for n in range(2):
-        settle(3, n)
-        settle(5, 2 + n)
-    plane_on(3)
     paired(2, 6)
     for n in range(2):
         settle(2, 2 + n)
         settle(6, n)
-    plane_on(5)
+    plane_on(3)
     for n in range(2):
         settle(2, n)
         settle(6, 2 + n)
-    plane_on(2)
+    plane_on(5)
     paired(1, 7)
     for n in range(2):
         settle(1, 2 + n)
         settle(7, n)
-    plane_on(6)
+    plane_on(2)
     for n in range(2):
         settle(1, n)
         settle(7, 2 + n)
+    plane_on(6)
     plane_on(1)
-    plane_on(7)
     paired(0)
     settle(0, 2, 3, 0, 1)
+    plane_on(7)
     total = plane_sum(0)
     for e in range(1, NZ):
         arrived("gz", e, zr.at[e])

time: 60 us -> 61.7 us (1.028)
  the two profiles are of different devices: /device:TPU:24 before, /device:TPU:16 now
where the time goes in v5:
time: 61.7 us; the launch traced here: 61.6 us
  Pallas kernels  59.6 us (97%)
  between operations  1.93 us (3%)
    pallas_call x1, Pallas kernels, shards(): pl.pallas_call(functools.partial(kernel, scale), out_shape=tuple((pltpu.V...  58.9 us

profile of v5, /device:TPU:16, one launch (start us, length us, event | category | flops | bytes accessed | tf_op | source)
XLA Modules:
  0.0 61.6 jit_solution(3224866595485270536)
XLA Ops:
  1.9 58.9 %shard_map.103 = (f32[128,384]{1,0:T(8,128)S(1)}, f32[2,64,64]{2,1,0:T(8,128)S(1)}, f32[2,64,64]{2,1,0:T(8,128)S(1)}) custom-call(bf16[128,384]{1,0:T(8,128)(2,1)} %tok.1, bf16[128,384]{1,0:T(8,128)(2,1)} %cot.1, bf16[2,64,64]{2,1,0:T(8,128)(2,1)} %bitcast.8, bf16[2,64,64]{2,1,0:T(8,128)(2,1)} %bitcast.9, s32[2,2]{1,0:T(2,128)} %bitcast.10, ...), custom_call_target="tpu_custom_call" | custom-call | flops 2013265920 | bytes 1048576 | tf_op jit(solution)/shard_map/pallas_call | solution.py:506
  60.8 0.7 %shard_map.104 = (f32[128,384]{1,0:T(8,128)}, f32[2,64,64]{2,1,0:T(8,128)}, f32[2,64,64]{2,1,0:T(8,128)}) custom-call(f32[128,384]{1,0:T(8,128)S(1)} %get-tuple-element.9.ig, f32[2,64,64]{2,1,0:T(8,128)S(1)} %get-tuple-element.10.g1, f32[2,64,64]{2,1,0:T(8,128)S(1)} %get-tuple-element.11.g2), custom_call_target="tpu_custom_call" | custom-call | tf_op jit(solution)/shard_map/pallas_call | solution.py:552
